TPU v7x, 32 devices: a whole 2x2x4 slice. The times are simulated.
32 devices in a mesh: blk: 8 (over z, y), dir: 4 (over x, core).
Axes of the slice: x: 2, y: 2, z: 4, core: 2. Of those that a mesh axis runs over, the one named last changes fastest.
Arguments:
- sky_map: float32 [4, 128, 8192], P('dir', 'blk'), may hold values from -6 to 6
- order_ids: int32 [32], replicated, may hold values from 0 to 4063, as said below
- legendre: float32 [32, 64, 128], P('blk'), may hold values from -0.5 to 0.5
- wigner: float32 [4, 32, 64, 128], P('dir', 'blk'), may hold values from -0.125 to 0.125
- wavelet: float32 [4, 64], P('dir'), may hold values from 0.5 to 1.5
- dir_ids: int32 [4], replicated, may hold values from 0 to 3, each once
Outputs:
- modulus: float32 [4, 4, 128, 8192], P('dir', None, 'blk')
Inputs may be any that keep to these rules, and one draw needn't show every extreme that they name: `order_ids`: distinct orders; the 4 slots of each index of blk hold pairs: its first 2 slots hold m values, its last 2 slots hold 4063 - m for the same m in order. `dir_ids`: a permutation.
All inputs are finite; a program needn't handle non-finite values.
Results may differ from a plain program's by a relative error of at most 0.0001.
Values sent between devices are 32-bit elements; how exact they have to be, the bound alone decides.
A program may use at most 64 MiB of HBM per device.

v0:
```python
import functools
import math

import jax
import jax.numpy as jnp
from jax import lax
from jax.experimental import pallas as pl
from jax.experimental.pallas import tpu as pltpu
from jax.sharding import PartitionSpec as P

L = 4096
INNER = 512
LANES = 128
MESH = pl.DeviceIdType.MESH


def sin_turn(phase, turn):
    quarter = turn // 4
    shifted = lax.bitwise_and(phase + quarter, turn - 1)
    folded = quarter - jnp.abs(shifted - 2 * quarter)
    u = folded.astype(jnp.float32) * (1.0 / quarter)
    square = u * u
    half = math.pi / 2
    total = jnp.full_like(u, -(half**11) / math.factorial(11))
    for power in (9, 7, 5, 3, 1):
        sign = 1.0 if power % 4 == 1 else -1.0
        total = total * square + sign * half**power / math.factorial(power)
    return total * u


def halves(value):
    high = value.astype(jnp.bfloat16)
    low = (value - high.astype(jnp.float32)).astype(jnp.bfloat16)
    return high, low


def iota(shape, dim):
    return lax.broadcasted_iota(jnp.int32, shape, dim)


def column_of(scalars, row, rows_of):
    value = jnp.full(row.shape, scalars[0], jnp.int32)
    for index in range(1, len(scalars)):
        value = jnp.where(rows_of(row) == index, scalars[index], value)
    return value


def dot(a, b, dims):
    return lax.dot_general(a, b, (dims, ((), ())), preferred_element_type=jnp.float32)


def spectra_kernel(
    blks, dirs, order_ref, dir_ref, sky_ref, legendre_ref, wigner_ref, wavelet_ref,
    mixed_ref, send1, recv1, send2, recv2, send_sem, recv_sem,
):
    blk, own = lax.axis_index("blk"), lax.axis_index("dir")
    devices = blks * dirs
    own_slot = own * blks + blk
    cycles, turn = sky_ref.shape[1], sky_ref.shape[2]
    orders, degrees, thetas = legendre_ref.shape
    steps = turn // INNER
    groups = LANES // cycles
    maps = dirs

    barrier = pltpu.get_barrier_semaphore()

    def greet(step, carry):
        other = lax.rem(own_slot + step, devices)
        pl.semaphore_signal(
            barrier, inc=1, device_id=(lax.rem(other, blks), lax.div(other, blks)),
            device_id_type=MESH,
        )
        return carry

    lax.fori_loop(1, devices, greet, 0)

    pieces = [sky_ref[0, :, a * INNER:(a + 1) * INNER] for a in range(steps)]
    sky_high, sky_low = halves(jnp.concatenate(pieces, axis=0))
    sky_both = jnp.concatenate([sky_high, sky_low], axis=0)
    rows = 2 * orders
    width = steps * cycles
    tile_row = iota((rows, LANES), 0)
    lane = iota((rows, LANES), 1)
    scale = 1.0 / math.sqrt(turn)

    def spectrum(group, carry):
        ids = []
        for j in range(groups):
            base = (group * groups + j) * orders
            ids.append(column_of(
                [order_ref[base + s] for s in range(orders)], tile_row,
                lambda r: lax.rem(r, orders),
            ))
        column = jnp.concatenate(ids, axis=0)
        tall = groups * rows
        part = lax.rem(lax.div(iota((tall, LANES), 0), orders), 2)
        offset = (1 + part) * (turn // 4)
        position = iota((tall, LANES), 1)
        table = jnp.concatenate(
            [sin_turn(column * (position + LANES * c) + offset, turn) for c in range(INNER // LANES)],
            axis=1,
        )
        table_high, table_low = halves(table)
        product = dot(jnp.concatenate([table_high, table_low], axis=0), sky_both, ((1,), (1,)))
        inner = product[:tall, :width] + product[:tall, width:] + product[tall:, :width]
        swapped = jnp.concatenate(
            [
                piece
                for j in range(groups)
                for piece in (
                    inner[j * rows + orders:(j + 1) * rows], inner[j * rows:j * rows + orders])
            ],
            axis=0,
        )
        total = jnp.zeros((tall, LANES), jnp.float32)
        for c in range(width // LANES):
            phase = column * (lax.div(position + LANES * c, cycles) * INNER)
            cut = slice(c * LANES, (c + 1) * LANES)
            total += sin_turn(phase + turn // 4, turn) * inner[:, cut]
            total += sin_turn(phase + part * (turn // 2), turn) * swapped[:, cut]
        shift = LANES // 2
        while shift >= cycles:
            total = total + pltpu.roll(total, shift, 1)
            shift //= 2
        total = total * scale
        for j in range(groups):
            block = jnp.where(lax.div(lane, cycles) == tile_row, total[j * rows:(j + 1) * rows], 0.0)
            send1[group * groups + j] = jnp.sum(block, axis=0, keepdims=True)
        return carry

    lax.fori_loop(0, blks // groups, spectrum, 0, unroll=blks == groups)

    pl.semaphore_wait(barrier, devices - 1)

    def scatter(send, recv, phase):
        def one(step, carry):
            other = lax.rem(own_slot + step, devices)
            other_blk, other_dir = lax.rem(other, blks), lax.div(other, blks)
            pltpu.make_async_remote_copy(
                src_ref=send.at[other_blk], dst_ref=recv.at[own_slot],
                send_sem=send_sem.at[phase], recv_sem=recv_sem.at[phase],
                device_id=(other_blk, other_dir), device_id_type=MESH,
            ).start()
            return carry

        lax.fori_loop(1, devices, one, 0)
        recv[own_slot] = send[blk]

    def settle(recv, sem, phase):
        span = recv.at[pl.ds(0, devices - 1)]
        pltpu.make_async_copy(span, span, sem.at[phase]).wait()

    scatter(send1, recv1, 0)

    flat = orders * degrees
    legendre_both = jnp.concatenate(halves(legendre_ref[...].reshape(flat, thetas)), axis=0)
    wigner_high, wigner_low = halves(wigner_ref[0].reshape(flat, thetas))
    tall = maps * rows
    own_ids = column_of(
        [order_ref[blk * orders + s] for s in range(orders)], iota((tall, flat), 0),
        lambda r: lax.rem(r, orders),
    )
    place = iota((tall, flat), 1)
    same = lax.div(place, degrees) == lax.rem(iota((tall, flat), 0), orders)
    live = L - degrees + lax.rem(place, degrees) >= own_ids
    weight = jnp.concatenate([wavelet_ref[...]] * orders, axis=1)
    weight = jnp.where(same & live, weight, 0.0)

    settle(recv1, recv_sem, 0)

    spectra = []
    for p in range(maps):
        chunks = []
        for g in range(blks // groups):
            start = p * blks + g * groups
            block = recv1[start:start + groups].reshape(groups, LANES)
            out = jnp.where(lax.div(lane, cycles) == tile_row, block, 0.0)
            for shift in range(1, groups):
                turned = pltpu.roll(pltpu.roll(block, groups - shift, 0), shift * cycles, 1)
                hit = lax.div(lane, cycles) == lax.rem(tile_row + shift, groups)
                out = jnp.where(hit, turned, out)
            chunks.append(out)
        spectra.append(jnp.concatenate(chunks, axis=1))
    both = jnp.concatenate(halves(jnp.concatenate(spectra, axis=0)), axis=0)
    product = dot(both, legendre_both, ((1,), (1,)))
    coeffs = product[:tall, :flat] + product[:tall, flat:] + product[tall:, :flat]
    both = jnp.concatenate(halves(coeffs * weight), axis=0)
    first = dot(both, wigner_high, ((1,), (0,)))
    second = dot(both[:tall], wigner_low, ((1,), (0,)))
    component = first[:tall] + first[tall:] + second

    for h in range(thetas // LANES):
        turned = [
            [
                block if shift == 0 else pltpu.roll(block, shift * cycles, 1)
                for shift in range(groups)
            ]
            for block in (
                component[p * rows:(p + 1) * rows, h * LANES:(h + 1) * LANES] for p in range(maps)
            )
        ]
        for j in range(groups):
            block = turned[0][(-j) % groups]
            for target in range(1, groups):
                block = jnp.where(
                    lax.div(lane, cycles) == target,
                    turned[target % maps][(target - j) % groups], block,
                )
            send2[h * groups + j] = jnp.where(
                lane[:orders] < LANES // 2, block[:orders], block[orders:]
            )

    scatter(send2, recv2, 1)

    direction = dir_ref[own]
    half_lane = iota((blks * orders, LANES), 1) < LANES // 2

    settle(recv2, recv_sem, 1)

    mixed = jnp.zeros((blks * orders, LANES), jnp.float32)
    for i in range(dirs):
        value = recv2[i * blks:(i + 1) * blks].reshape(blks * orders, LANES)
        azimuth = 2 * i - dirs + 1
        phase = jnp.full((1, LANES), direction, jnp.int32) * (azimuth * (turn // (2 * dirs)))
        phase = phase + 4 * turn
        sine = sin_turn(phase, turn)
        mixed += sin_turn(phase + turn // 4, turn) * value
        mixed += jnp.where(half_lane, -sine, sine) * pltpu.roll(value, LANES // 2, 1)
    mixed_ref[...] = mixed

    settle(recv1, send_sem, 0)
    settle(recv2, send_sem, 1)


def maps_kernel(turn, maps, cycles, order_ref, mixed_ref, out_ref, total):
    slab = 32
    steps = turn // INNER
    chunks = mixed_ref.shape[0] // slab
    row = iota((8, LANES), 0)
    lane = iota((slab, LANES), 1)
    real = lane < LANES // 2

    def maps_of(chunk, last):
        column = jnp.concatenate(
            [
                column_of(
                    [order_ref[chunk * slab + q * 8 + s] for s in range(8)], row, lambda r: r)
                for q in range(slab // 8)
            ],
            axis=0,
        )
        phases = [column * (lane + LANES * c) for c in range(INNER // LANES)]
        cosine = jnp.concatenate([sin_turn(x + turn // 4, turn) for x in phases], axis=1)
        sine = jnp.concatenate([sin_turn(x, turn) for x in phases], axis=1)
        table = jnp.concatenate(
            [
                jnp.concatenate([cosine, sine], axis=1),
                jnp.concatenate([-sine, cosine], axis=1),
            ],
            axis=0,
        )
        table_high, table_low = halves(table)
        right = jnp.concatenate([table_high, table_high, table_low], axis=0)
        turns = [mixed_ref[pl.ds(chunk * slab, slab), :]]
        while len(turns) < steps:
            phase = column * (INNER * len(turns))
            across = sin_turn(phase + turn // 4, turn)
            sine_a = sin_turn(phase, turn)
            sine_a = jnp.where(real, -sine_a, sine_a)
            turns = turns + [
                across * value + sine_a * pltpu.roll(value, LANES // 2, 1) for value in turns
            ]
        for pair in range(steps // 2):
            one, two = turns[2 * pair], turns[2 * pair + 1]
            left = jnp.concatenate(
                [
                    jnp.where(real, one, pltpu.roll(two, LANES // 2, 1)),
                    jnp.where(real, pltpu.roll(one, LANES // 2, 1), two),
                ],
                axis=0,
            )
            left_high, left_low = halves(left)
            left = jnp.concatenate([left_high, left_low, left_high], axis=0)
            value = dot(left, right, ((0,), (0,)))
            if chunks > 1:
                value = value + total[pair]
                total[pair] = value
            if last:
                real_part, imag_part = value[:, :INNER], value[:, INNER:]
                modulus = jnp.sqrt(real_part * real_part + imag_part * imag_part)
                half = maps * cycles
                for part in range(2):
                    a = 2 * pair + part
                    out_ref[0, :, :, a * INNER:(a + 1) * INNER] = modulus[
                        part * half:(part + 1) * half
                    ].reshape(maps, cycles, INNER)

    if chunks > 1:
        total[...] = jnp.zeros_like(total)

        def partial(chunk, carry):
            maps_of(chunk, False)
            return carry

        lax.fori_loop(0, chunks - 1, partial, 0)
    maps_of(chunks - 1, True)


def local(blks, dirs, sky_map, order_ids, legendre, wigner, wavelet, dir_ids):
    devices = blks * dirs
    cycles, turn = sky_map.shape[1:]
    orders = legendre.shape[0]
    vmem = pl.BlockSpec(memory_space=pltpu.VMEM)
    smem = pl.BlockSpec(memory_space=pltpu.SMEM)
    mixed = pl.pallas_call(
        functools.partial(spectra_kernel, blks, dirs),
        out_shape=jax.ShapeDtypeStruct((blks * orders, LANES), jnp.float32),
        in_specs=[smem, smem, vmem, vmem, vmem, vmem],
        out_specs=vmem,
        scratch_shapes=[
            pltpu.VMEM((blks, 1, LANES), jnp.float32),
            pltpu.VMEM((devices, 1, LANES), jnp.float32),
            pltpu.VMEM((blks, orders, LANES), jnp.float32),
            pltpu.VMEM((devices, orders, LANES), jnp.float32),
            pltpu.SemaphoreType.DMA((2,)),
            pltpu.SemaphoreType.DMA((2,)),
        ],
        compiler_params=pltpu.CompilerParams(
            collective_id=0, has_side_effects=True, vmem_limit_bytes=48 * 2**20
        ),
    )(order_ids, dir_ids, sky_map, legendre, wigner, wavelet)
    several = blks * orders > 32
    total_shape = (turn // INNER // 2, LANES, 2 * INNER) if several else (1, 8, LANES)
    return pl.pallas_call(
        functools.partial(maps_kernel, turn, dirs, cycles),
        out_shape=jax.ShapeDtypeStruct((1, dirs, cycles, turn), jnp.float32),
        in_specs=[smem, vmem],
        out_specs=vmem,
        scratch_shapes=[pltpu.VMEM(total_shape, jnp.float32)],
        compiler_params=pltpu.CompilerParams(vmem_limit_bytes=48 * 2**20),
    )(order_ids, mixed)


def solution(mesh):
    return jax.shard_map(
        functools.partial(local, mesh.shape["blk"], mesh.shape["dir"]),
        mesh=mesh,
        in_specs=(
            P("dir", "blk", None),
            P(),
            P("blk", None, None),
            P("dir", "blk", None, None),
            P("dir", None),
            P(),
        ),
        out_specs=P("dir", None, "blk", None),
        check_vma=False,
    )
```

profile of v0, /device:TPU:0, one launch (start us, length us, event | category | flops | bytes accessed | tf_op | source)
XLA Modules:
  0.0 25.2 jit_solution(11296614480565010923)
XLA Ops:
  0.0 0.0 copy-start
  0.0 1.0 %copy-done = f32[1,16,8192]{2,1,0:T(8,128)S(1)} copy-done((f32[1,16,8192]{2,1,0:T(8,128)S(1)}, f32[1,16,8192]{2,1,0:T(8,128)}, u32[]{:S(2)}) %copy-start) | copy-done | bytes 524312
  1.0 0.0 copy-start.1
  1.0 0.9 %copy-done.1 = f32[4,64,128]{2,1,0:T(8,128)S(1)} copy-done((f32[4,64,128]{2,1,0:T(8,128)S(1)}, f32[4,64,128]{2,1,0:T(8,128)}, u32[]{:S(2)}) %copy-start.1) | copy-done | bytes 131096
  1.9 0.0 copy-start.2
  1.9 0.9 %copy-done.2 = f32[1,4,64,128]{3,2,1,0:T(8,128)S(1)} copy-done((f32[1,4,64,128]{3,2,1,0:T(8,128)S(1)}, f32[1,4,64,128]{3,2,1,0:T(8,128)}, u32[]{:S(2)}) %copy-start.2) | copy-done | bytes 131096
  2.9 0.0 copy-start.3
  2.9 0.7 %copy-done.3 = s32[32]{0:T(128)S(1)} copy-done((s32[32]{0:T(128)S(1)}, s32[32]{0:T(128)}, u32[]{:S(2)}) %copy-start.3) | copy-done | bytes 152
  3.5 0.0 copy-start.4
  3.5 0.7 %copy-done.4 = s32[4]{0:T(128)S(1)} copy-done((s32[4]{0:T(128)S(1)}, s32[4]{0:T(128)}, u32[]{:S(2)}) %copy-start.4) | copy-done | bytes 40
  4.2 0.0 copy-start.5
  4.2 0.7 %copy-done.5 = f32[1,64]{1,0:T(1,128)S(1)} copy-done((f32[1,64]{1,0:T(1,128)S(1)}, f32[1,64]{1,0:T(1,128)}, u32[]{:S(2)}) %copy-start.5) | copy-done | bytes 280
  4.8 17.2 %shard_map.64.mixed_ref = f32[32,128]{1,0:T(8,128)S(1)} custom-call(s32[32]{0:T(128)S(1)} %copy-done.3, s32[4]{0:T(128)S(1)} %copy-done.4, f32[1,16,8192]{2,1,0:T(8,128)S(1)} %copy-done, f32[4,64,128]{2,1,0:T(8,128)S(1)} %copy-done.1, f32[1,4,64,128]{3,2,1,0:T(8,128)S(1)} %copy-done.2, f32[1,64]{1,0:T(1,128)S(1)} %copy-done.5), custom_call_target="tpu_custom_call" | custom-call | tf_op jit(solution)/shard_map/pallas_call | solution.py:315
  22.0 3.2 %shard_map.65 = f32[1,4,16,8192]{3,2,1,0:T(8,128)} custom-call(s32[32]{0:T(128)S(1)} %copy-done.3, f32[32,128]{1,0:T(8,128)S(1)} %shard_map.64.mixed_ref), custom_call_target="tpu_custom_call" | custom-call | tf_op jit(solution)/shard_map/pallas_call | solution.py:334
Async XLA Ops:
  0.0 1.0 %copy-start = (f32[1,16,8192]{2,1,0:T(8,128)S(1)}, f32[1,16,8192]{2,1,0:T(8,128)}, u32[]{:S(2)}) copy-start(f32[1,16,8192]{2,1,0:T(8,128)} %sky_ref.1) | copy-start | bytes 1572868
  1.0 0.9 %copy-start.1 = (f32[4,64,128]{2,1,0:T(8,128)S(1)}, f32[4,64,128]{2,1,0:T(8,128)}, u32[]{:S(2)}) copy-start(f32[4,64,128]{2,1,0:T(8,128)} %legendre_ref.1) | copy-start | bytes 393220
  1.9 0.9 %copy-start.2 = (f32[1,4,64,128]{3,2,1,0:T(8,128)S(1)}, f32[1,4,64,128]{3,2,1,0:T(8,128)}, u32[]{:S(2)}) copy-start(f32[1,4,64,128]{3,2,1,0:T(8,128)} %wigner_ref.1) | copy-start | bytes 393220
  2.9 0.7 %copy-start.3 = (s32[32]{0:T(128)S(1)}, s32[32]{0:T(128)}, u32[]{:S(2)}) copy-start(s32[32]{0:T(128)} %order_ref.3) | copy-start | bytes 388
  3.5 0.7 %copy-start.4 = (s32[4]{0:T(128)S(1)}, s32[4]{0:T(128)}, u32[]{:S(2)}) copy-start(s32[4]{0:T(128)} %dir_ref.1) | copy-start | bytes 52
  4.2 0.7 %copy-start.5 = (f32[1,64]{1,0:T(1,128)S(1)}, f32[1,64]{1,0:T(1,128)}, u32[]{:S(2)}) copy-start(f32[1,64]{1,0:T(1,128)} %wavelet_ref.1) | copy-start | bytes 772
where the time goes:
time: 25.4 us; the launch traced here: 25.2 us
  Pallas kernels  20.4 us (80%)
  local copies, waits for them, and re-layouts  4.81 us (19%)
    pallas_call x1, Pallas kernels, local(): pl.pallas_call(functools.partial(spectra_kernel, blks, dirs), out_shape=j...  17.2 us
    unnamed x12, local copies, waits for them, and re-layouts  4.81 us
    pallas_call x1, Pallas kernels, local(): pl.pallas_call(functools.partial(maps_kernel, turn, dirs, cycles), out_sh...  3.2 us

commit v1 on v0

--- a/solution.py
+++ b/solution.py
@@ -50,9 +50,19 @@
 
 
 def spectra_kernel(
-    blks, dirs, order_ref, dir_ref, sky_ref, legendre_ref, wigner_ref, wavelet_ref,
-    mixed_ref, send1, recv1, send2, recv2, send_sem, recv_sem,
+    blks, dirs, order_hbm, dir_hbm, sky_hbm, legendre_hbm, wigner_hbm, wavelet_hbm,
+    mixed_ref, column_ref, order_ref, dir_ref, sky_ref, legendre_ref, wigner_ref, wavelet_ref,
+    send1, recv1, send2, recv2, in_sem, send_sem, recv_sem,
 ):
+    loads = [
+        pltpu.make_async_copy(source, target, in_sem.at[index])
+        for index, (source, target) in enumerate((
+            (order_hbm, order_ref), (sky_hbm, sky_ref), (dir_hbm, dir_ref),
+            (legendre_hbm, legendre_ref), (wigner_hbm, wigner_ref), (wavelet_hbm, wavelet_ref),
+        ))
+    ]
+    for load in loads:
+        load.start()
     blk, own = lax.axis_index("blk"), lax.axis_index("dir")
     devices = blks * dirs
     own_slot = own * blks + blk
@@ -74,6 +84,8 @@
 
     lax.fori_loop(1, devices, greet, 0)
 
+    loads[0].wait()
+    loads[1].wait()
     pieces = [sky_ref[0, :, a * INNER:(a + 1) * INNER] for a in range(steps)]
     sky_high, sky_low = halves(jnp.concatenate(pieces, axis=0))
     sky_both = jnp.concatenate([sky_high, sky_low], axis=0)
@@ -152,6 +164,8 @@
 
     scatter(send1, recv1, 0)
 
+    for load in loads[2:]:
+        load.wait()
     flat = orders * degrees
     legendre_both = jnp.concatenate(halves(legendre_ref[...].reshape(flat, thetas)), axis=0)
     wigner_high, wigner_low = halves(wigner_ref[0].reshape(flat, thetas))
@@ -212,6 +226,15 @@
 
     scatter(send2, recv2, 1)
 
+    def put_columns(chunk, carry):
+        for q in range(groups * orders // 8):
+            base = chunk * groups * orders + 8 * q
+            column_ref[pl.ds(pl.multiple_of(base, 8), 8), :] = column_of(
+                [order_ref[base + s] for s in range(8)], tile_row, lambda r: r)
+        return carry
+
+    lax.fori_loop(0, blks // groups, put_columns, 0, unroll=blks == groups)
+
     direction = dir_ref[own]
     half_lane = iota((blks * orders, LANES), 1) < LANES // 2
 
@@ -232,23 +255,15 @@
     settle(recv2, send_sem, 1)
 
 
-def maps_kernel(turn, maps, cycles, order_ref, mixed_ref, out_ref, total):
+def maps_kernel(turn, maps, cycles, column_ref, mixed_ref, out_ref, total):
     slab = 32
     steps = turn // INNER
     chunks = mixed_ref.shape[0] // slab
-    row = iota((8, LANES), 0)
     lane = iota((slab, LANES), 1)
     real = lane < LANES // 2
 
     def maps_of(chunk, last):
-        column = jnp.concatenate(
-            [
-                column_of(
-                    [order_ref[chunk * slab + q * 8 + s] for s in range(8)], row, lambda r: r)
-                for q in range(slab // 8)
-            ],
-            axis=0,
-        )
+        column = column_ref[pl.ds(chunk * slab, slab), :]
         phases = [column * (lane + LANES * c) for c in range(INNER // LANES)]
         cosine = jnp.concatenate([sin_turn(x + turn // 4, turn) for x in phases], axis=1)
         sine = jnp.concatenate([sin_turn(x, turn) for x in phases], axis=1)
@@ -311,17 +326,26 @@
     cycles, turn = sky_map.shape[1:]
     orders = legendre.shape[0]
     vmem = pl.BlockSpec(memory_space=pltpu.VMEM)
-    smem = pl.BlockSpec(memory_space=pltpu.SMEM)
-    mixed = pl.pallas_call(
+    hbm = pl.BlockSpec(memory_space=pltpu.HBM)
+    slots = jax.ShapeDtypeStruct((blks * orders, LANES), jnp.float32)
+    sky_map, legendre, wigner, wavelet, order_ids, dir_ids = (pltpu.with_memory_space_constraint(x, pltpu.HBM) for x in (sky_map, legendre, wigner, wavelet, order_ids, dir_ids))
+    mixed, columns = pl.pallas_call(
         functools.partial(spectra_kernel, blks, dirs),
-        out_shape=jax.ShapeDtypeStruct((blks * orders, LANES), jnp.float32),
-        in_specs=[smem, smem, vmem, vmem, vmem, vmem],
-        out_specs=vmem,
+        out_shape=(slots, jax.ShapeDtypeStruct(slots.shape, jnp.int32)),
+        in_specs=[hbm] * 6,
+        out_specs=(vmem, vmem),
         scratch_shapes=[
+            pltpu.SMEM(order_ids.shape, jnp.int32),
+            pltpu.SMEM(dir_ids.shape, jnp.int32),
+            pltpu.VMEM(sky_map.shape, jnp.float32),
+            pltpu.VMEM(legendre.shape, jnp.float32),
+            pltpu.VMEM(wigner.shape, jnp.float32),
+            pltpu.VMEM(wavelet.shape, jnp.float32),
             pltpu.VMEM((blks, 1, LANES), jnp.float32),
             pltpu.VMEM((devices, 1, LANES), jnp.float32),
             pltpu.VMEM((blks, orders, LANES), jnp.float32),
             pltpu.VMEM((devices, orders, LANES), jnp.float32),
+            pltpu.SemaphoreType.DMA((6,)),
             pltpu.SemaphoreType.DMA((2,)),
             pltpu.SemaphoreType.DMA((2,)),
         ],
@@ -334,11 +358,11 @@
     return pl.pallas_call(
         functools.partial(maps_kernel, turn, dirs, cycles),
         out_shape=jax.ShapeDtypeStruct((1, dirs, cycles, turn), jnp.float32),
-        in_specs=[smem, vmem],
+        in_specs=[vmem, vmem],
         out_specs=vmem,
         scratch_shapes=[pltpu.VMEM(total_shape, jnp.float32)],
         compiler_params=pltpu.CompilerParams(vmem_limit_bytes=48 * 2**20),
-    )(order_ids, mixed)
+    )(columns, mixed)
 
 
 def solution(mesh):

time: 25.4 us -> 19.4 us (0.76)
  local copies, waits for them, and re-layouts: 4.81 us -> 0 us
  Pallas kernels: 20.4 us -> 19.2 us
    unnamed x12 -> x0, local copies, waits for them, and re-layouts: 4.81 us -> none
    pallas_call x1, Pallas kernels: 17.2 us -> 16.6 us  [local(): pl.pallas_call(functools.partial(spectra_kernel, blks, dirs), out_shape=(...]
    pallas_call x1, Pallas kernels: 3.2 us -> 2.65 us  [local(): pl.pallas_call(functools.partial(maps_kernel, turn, dirs, cycles), out_sh...]
where the time goes in v1:
time: 19.4 us; the launch traced here: 19.2 us
  Pallas kernels  19.2 us (99%)
    pallas_call x1, Pallas kernels, local(): pl.pallas_call(functools.partial(spectra_kernel, blks, dirs), out_shape=(...  16.6 us
    pallas_call x1, Pallas kernels, local(): pl.pallas_call(functools.partial(maps_kernel, turn, dirs, cycles), out_sh...  2.65 us

profile of v1, /device:TPU:0, one launch (start us, length us, event | category | flops | bytes accessed | tf_op | source)
XLA Modules:
  0.0 19.2 jit_solution(8066563073897862020)
XLA Ops:
  0.0 16.6 %shard_map.64 = (f32[32,128]{1,0:T(8,128)S(1)}, s32[32,128]{1,0:T(8,128)S(1)}) custom-call(s32[32]{0:T(128)} %order_hbm.1, s32[4]{0:T(128)} %dir_hbm.1, f32[1,16,8192]{2,1,0:T(8,128)} %sky_hbm.1, f32[4,64,128]{2,1,0:T(8,128)} %legendre_hbm.1, f32[1,4,64,128]{3,2,1,0:T(8,128)} %wigner_hbm.1, f32[1,64]{1,0:T(1,128)} %wavelet_hbm.1), custom_call_target="tpu_custom_call" | custom-call | tf_op jit(solution)/shard_map/pallas_call | solution.py:332
  16.6 2.6 %shard_map.65 = f32[1,4,16,8192]{3,2,1,0:T(8,128)} custom-call(s32[32,128]{1,0:T(8,128)S(1)} %get-tuple-element.7.column_ref, f32[32,128]{1,0:T(8,128)S(1)} %get-tuple-element.8.mixed_ref), custom_call_target="tpu_custom_call" | custom-call | tf_op jit(solution)/shard_map/pallas_call | solution.py:358

commit v2 on v0

--- a/solution.py
+++ b/solution.py
@@ -50,8 +50,9 @@
 
 
 def spectra_kernel(
-    blks, dirs, order_ref, dir_ref, sky_ref, legendre_ref, wigner_ref, wavelet_ref,
-    mixed_ref, send1, recv1, send2, recv2, send_sem, recv_sem,
+    blks, dirs, order_hbm, dir_hbm, sky_hbm, legendre_hbm, wigner_hbm, wavelet_hbm,
+    mixed_ref, table_ref, turn_ref, order_ref, dir_ref, sky_ref, legendre_ref, wigner_ref, wavelet_ref,
+    send1, recv1, send2, recv2, in_sem, send_sem, recv_sem,
 ):
     blk, own = lax.axis_index("blk"), lax.axis_index("dir")
     devices = blks * dirs
@@ -64,16 +65,33 @@
 
     barrier = pltpu.get_barrier_semaphore()
 
-    def greet(step, carry):
-        other = lax.rem(own_slot + step, devices)
+    power = devices & (devices - 1) == 0
+
+    def partner(step):
+        place = blk * dirs + own
+        other = lax.bitwise_xor(place, devices - step) if power else lax.rem(place + step, devices)
+        return lax.div(other, dirs), lax.rem(other, dirs)
+
+    def for_partners(body):
+        lax.fori_loop(1, devices, lambda step, carry: body(*partner(step)), None, unroll=1)
+
+    def greet(other_blk, other_dir):
         pl.semaphore_signal(
-            barrier, inc=1, device_id=(lax.rem(other, blks), lax.div(other, blks)),
-            device_id_type=MESH,
-        )
-        return carry
-
-    lax.fori_loop(1, devices, greet, 0)
-
+            barrier, inc=1, device_id=(other_blk, other_dir), device_id_type=MESH)
+
+    for_partners(greet)
+    loads = [
+        pltpu.make_async_copy(source, target, in_sem.at[index])
+        for index, (source, target) in enumerate((
+            (order_hbm, order_ref), (sky_hbm, sky_ref), (dir_hbm, dir_ref),
+            (legendre_hbm, legendre_ref), (wigner_hbm, wigner_ref), (wavelet_hbm, wavelet_ref),
+        ))
+    ]
+    for load in loads:
+        load.start()
+
+    loads[0].wait()
+    loads[1].wait()
     pieces = [sky_ref[0, :, a * INNER:(a + 1) * INNER] for a in range(steps)]
     sky_high, sky_low = halves(jnp.concatenate(pieces, axis=0))
     sky_both = jnp.concatenate([sky_high, sky_low], axis=0)
@@ -133,17 +151,14 @@
     pl.semaphore_wait(barrier, devices - 1)
 
     def scatter(send, recv, phase):
-        def one(step, carry):
-            other = lax.rem(own_slot + step, devices)
-            other_blk, other_dir = lax.rem(other, blks), lax.div(other, blks)
+        def one(other_blk, other_dir):
             pltpu.make_async_remote_copy(
                 src_ref=send.at[other_blk], dst_ref=recv.at[own_slot],
                 send_sem=send_sem.at[phase], recv_sem=recv_sem.at[phase],
                 device_id=(other_blk, other_dir), device_id_type=MESH,
             ).start()
-            return carry
-
-        lax.fori_loop(1, devices, one, 0)
+
+        for_partners(one)
         recv[own_slot] = send[blk]
 
     def settle(recv, sem, phase):
@@ -152,6 +167,8 @@
 
     scatter(send1, recv1, 0)
 
+    for load in loads[2:]:
+        load.wait()
     flat = orders * degrees
     legendre_both = jnp.concatenate(halves(legendre_ref[...].reshape(flat, thetas)), axis=0)
     wigner_high, wigner_low = halves(wigner_ref[0].reshape(flat, thetas))
@@ -212,44 +229,20 @@
 
     scatter(send2, recv2, 1)
 
-    direction = dir_ref[own]
-    half_lane = iota((blks * orders, LANES), 1) < LANES // 2
-
-    settle(recv2, recv_sem, 1)
-
-    mixed = jnp.zeros((blks * orders, LANES), jnp.float32)
-    for i in range(dirs):
-        value = recv2[i * blks:(i + 1) * blks].reshape(blks * orders, LANES)
-        azimuth = 2 * i - dirs + 1
-        phase = jnp.full((1, LANES), direction, jnp.int32) * (azimuth * (turn // (2 * dirs)))
-        phase = phase + 4 * turn
-        sine = sin_turn(phase, turn)
-        mixed += sin_turn(phase + turn // 4, turn) * value
-        mixed += jnp.where(half_lane, -sine, sine) * pltpu.roll(value, LANES // 2, 1)
-    mixed_ref[...] = mixed
-
-    settle(recv1, send_sem, 0)
-    settle(recv2, send_sem, 1)
-
-
-def maps_kernel(turn, maps, cycles, order_ref, mixed_ref, out_ref, total):
-    slab = 32
-    steps = turn // INNER
-    chunks = mixed_ref.shape[0] // slab
-    row = iota((8, LANES), 0)
-    lane = iota((slab, LANES), 1)
-    real = lane < LANES // 2
-
-    def maps_of(chunk, last):
+    slab = groups * orders
+    levels = (steps - 1).bit_length()
+
+    def put_tables(chunk, carry):
         column = jnp.concatenate(
             [
                 column_of(
-                    [order_ref[chunk * slab + q * 8 + s] for s in range(8)], row, lambda r: r)
+                    [order_ref[chunk * slab + 8 * q + s] for s in range(8)], tile_row, lambda r: r)
                 for q in range(slab // 8)
             ],
             axis=0,
         )
-        phases = [column * (lane + LANES * c) for c in range(INNER // LANES)]
+        place = iota((slab, LANES), 1)
+        phases = [column * (place + LANES * c) for c in range(INNER // LANES)]
         cosine = jnp.concatenate([sin_turn(x + turn // 4, turn) for x in phases], axis=1)
         sine = jnp.concatenate([sin_turn(x, turn) for x in phases], axis=1)
         table = jnp.concatenate(
@@ -260,15 +253,61 @@
             axis=0,
         )
         table_high, table_low = halves(table)
-        right = jnp.concatenate([table_high, table_high, table_low], axis=0)
+        tall = 6 * slab
+        table_ref[pl.ds(pl.multiple_of(chunk * tall, tall), tall), :] = jnp.concatenate(
+            [table_high, table_high, table_low], axis=0)
+        for level in range(levels):
+            phase = column * (INNER << level)
+            sine = sin_turn(phase, turn)
+            turn_ref[chunk, 2 * level] = sin_turn(phase + turn // 4, turn)
+            turn_ref[chunk, 2 * level + 1] = jnp.where(place < LANES // 2, -sine, sine)
+        return carry
+
+    lax.fori_loop(0, blks // groups, put_tables, 0, unroll=blks == groups)
+
+    direction = dir_ref[own]
+    half_lane = iota((blks * orders, LANES), 1) < LANES // 2
+
+    factors = []
+    for i in range(dirs):
+        azimuth = 2 * i - dirs + 1
+        phase = jnp.full((blks * orders, LANES), direction, jnp.int32)
+        phase = phase * (azimuth * (turn // (2 * dirs))) + 4 * turn
+        sine = sin_turn(phase, turn)
+        factors.append((sin_turn(phase + turn // 4, turn), jnp.where(half_lane, sine, -sine)))
+
+    settle(recv2, recv_sem, 1)
+
+    mixed = jnp.zeros((blks * orders, LANES), jnp.float32)
+    crossed = jnp.zeros((blks * orders, LANES), jnp.float32)
+    for i, (along, across) in enumerate(factors):
+        value = recv2[i * blks:(i + 1) * blks].reshape(blks * orders, LANES)
+        mixed += along * value
+        crossed += across * value
+    mixed = mixed + pltpu.roll(crossed, LANES // 2, 1)
+    mixed_ref[...] = mixed
+
+    settle(recv1, send_sem, 0)
+    settle(recv2, send_sem, 1)
+
+
+def maps_kernel(turn, maps, cycles, mixed_ref, table_ref, turn_ref, out_hbm, out_ref, total, out_sem):
+    slab = 32
+    steps = turn // INNER
+    chunks = mixed_ref.shape[0] // slab
+    lane = iota((slab, LANES), 1)
+    real = lane < LANES // 2
+    writes = []
+
+    def maps_of(chunk, last):
+        tall = 6 * slab
+        right = table_ref[pl.ds(pl.multiple_of(chunk * tall, tall), tall), :]
         turns = [mixed_ref[pl.ds(chunk * slab, slab), :]]
         while len(turns) < steps:
-            phase = column * (INNER * len(turns))
-            across = sin_turn(phase + turn // 4, turn)
-            sine_a = sin_turn(phase, turn)
-            sine_a = jnp.where(real, -sine_a, sine_a)
+            level = 2 * (len(turns).bit_length() - 1)
+            along, across = turn_ref[chunk, level], turn_ref[chunk, level + 1]
             turns = turns + [
-                across * value + sine_a * pltpu.roll(value, LANES // 2, 1) for value in turns
+                along * value + across * pltpu.roll(value, LANES // 2, 1) for value in turns
             ]
         for pair in range(steps // 2):
             one, two = turns[2 * pair], turns[2 * pair + 1]
@@ -287,13 +326,19 @@
                 total[pair] = value
             if last:
                 real_part, imag_part = value[:, :INNER], value[:, INNER:]
-                modulus = jnp.sqrt(real_part * real_part + imag_part * imag_part)
+                power = real_part * real_part + imag_part * imag_part
+                modulus = power * lax.rsqrt(jnp.maximum(power, 1e-37))
                 half = maps * cycles
                 for part in range(2):
                     a = 2 * pair + part
                     out_ref[0, :, :, a * INNER:(a + 1) * INNER] = modulus[
                         part * half:(part + 1) * half
                     ].reshape(maps, cycles, INNER)
+                cut = pl.ds(2 * pair * INNER, 2 * INNER)
+                write = pltpu.make_async_copy(
+                    out_ref.at[:, :, :, cut], out_hbm.at[:, :, :, cut], out_sem.at[pair])
+                write.start()
+                writes.append(write)
 
     if chunks > 1:
         total[...] = jnp.zeros_like(total)
@@ -304,6 +349,8 @@
 
         lax.fori_loop(0, chunks - 1, partial, 0)
     maps_of(chunks - 1, True)
+    for write in writes:
+        write.wait()
 
 
 def local(blks, dirs, sky_map, order_ids, legendre, wigner, wavelet, dir_ids):
@@ -311,17 +358,31 @@
     cycles, turn = sky_map.shape[1:]
     orders = legendre.shape[0]
     vmem = pl.BlockSpec(memory_space=pltpu.VMEM)
-    smem = pl.BlockSpec(memory_space=pltpu.SMEM)
-    mixed = pl.pallas_call(
+    hbm = pl.BlockSpec(memory_space=pltpu.HBM)
+    slots = jax.ShapeDtypeStruct((blks * orders, LANES), jnp.float32)
+    sky_map, legendre, wigner, wavelet, order_ids, dir_ids = (pltpu.with_memory_space_constraint(x, pltpu.HBM) for x in (sky_map, legendre, wigner, wavelet, order_ids, dir_ids))
+    slab = LANES // cycles * orders
+    chunks = blks * orders // slab
+    table = jax.ShapeDtypeStruct((chunks * 6 * slab, 2 * INNER), jnp.bfloat16)
+    levels = (turn // INNER - 1).bit_length()
+    turns = jax.ShapeDtypeStruct((chunks, 2 * levels, slab, LANES), jnp.float32)
+    middle = pl.pallas_call(
         functools.partial(spectra_kernel, blks, dirs),
-        out_shape=jax.ShapeDtypeStruct((blks * orders, LANES), jnp.float32),
-        in_specs=[smem, smem, vmem, vmem, vmem, vmem],
-        out_specs=vmem,
+        out_shape=(slots, table, turns),
+        in_specs=[hbm] * 6,
+        out_specs=(vmem, vmem, vmem),
         scratch_shapes=[
+            pltpu.SMEM(order_ids.shape, jnp.int32),
+            pltpu.SMEM(dir_ids.shape, jnp.int32),
+            pltpu.VMEM(sky_map.shape, jnp.float32),
+            pltpu.VMEM(legendre.shape, jnp.float32),
+            pltpu.VMEM(wigner.shape, jnp.float32),
+            pltpu.VMEM(wavelet.shape, jnp.float32),
             pltpu.VMEM((blks, 1, LANES), jnp.float32),
             pltpu.VMEM((devices, 1, LANES), jnp.float32),
             pltpu.VMEM((blks, orders, LANES), jnp.float32),
             pltpu.VMEM((devices, orders, LANES), jnp.float32),
+            pltpu.SemaphoreType.DMA((6,)),
             pltpu.SemaphoreType.DMA((2,)),
             pltpu.SemaphoreType.DMA((2,)),
         ],
@@ -329,16 +390,21 @@
             collective_id=0, has_side_effects=True, vmem_limit_bytes=48 * 2**20
         ),
     )(order_ids, dir_ids, sky_map, legendre, wigner, wavelet)
-    several = blks * orders > 32
+    several = chunks > 1
     total_shape = (turn // INNER // 2, LANES, 2 * INNER) if several else (1, 8, LANES)
+    out = jax.ShapeDtypeStruct((1, dirs, cycles, turn), jnp.float32)
     return pl.pallas_call(
         functools.partial(maps_kernel, turn, dirs, cycles),
-        out_shape=jax.ShapeDtypeStruct((1, dirs, cycles, turn), jnp.float32),
-        in_specs=[smem, vmem],
-        out_specs=vmem,
-        scratch_shapes=[pltpu.VMEM(total_shape, jnp.float32)],
+        out_shape=out,
+        in_specs=[vmem] * 3,
+        out_specs=hbm,
+        scratch_shapes=[
+            pltpu.VMEM(out.shape, jnp.float32),
+            pltpu.VMEM(total_shape, jnp.float32),
+            pltpu.SemaphoreType.DMA((turn // INNER // 2,)),
+        ],
         compiler_params=pltpu.CompilerParams(vmem_limit_bytes=48 * 2**20),
-    )(order_ids, mixed)
+    )(*middle)
 
 
 def solution(mesh):

time: 25.4 us -> 18.5 us (0.73)
  local copies, waits for them, and re-layouts: 4.81 us -> 0 us
  Pallas kernels: 20.4 us -> 18.3 us
    unnamed x12 -> x0, local copies, waits for them, and re-layouts: 4.81 us -> none
    pallas_call x1, Pallas kernels: 3.2 us -> 1.99 us  [local(): pl.pallas_call(functools.partial(maps_kernel, turn, dirs, cycles), out_sh...]
    pallas_call x1, Pallas kernels: 17.2 us -> 16.3 us  [local(): pl.pallas_call(functools.partial(spectra_kernel, blks, dirs), out_shape=(...]
where the time goes in v2:
time: 18.5 us; the launch traced here: 18.3 us
  Pallas kernels  18.3 us (99%)
    pallas_call x1, Pallas kernels, local(): pl.pallas_call(functools.partial(spectra_kernel, blks, dirs), out_shape=(...  16.3 us
    pallas_call x1, Pallas kernels, local(): pl.pallas_call(functools.partial(maps_kernel, turn, dirs, cycles), out_sh...  1.99 us

profile of v2, /device:TPU:0, one launch (start us, length us, event | category | flops | bytes accessed | tf_op | source)
XLA Modules:
  0.0 18.3 jit_solution(9172593679533078402)
XLA Ops:
  0.0 16.3 %shard_map.64 = (f32[32,128]{1,0:T(8,128)S(1)}, bf16[192,1024]{1,0:T(8,128)(2,1)S(1)}, f32[1,8,32,128]{3,2,1,0:T(8,128)S(1)}) custom-call(s32[32]{0:T(128)} %order_hbm.1, s32[4]{0:T(128)} %dir_hbm.1, f32[1,16,8192]{2,1,0:T(8,128)} %sky_hbm.1, f32[4,64,128]{2,1,0:T(8,128)} %legendre_hbm.1, f32[1,4,64,128]{3,2,1,0:T(8,128)} %wigner_hbm.1, f32[1,64]{1,0:T(1,128)} %wavelet_hbm.1), custom_call_target="tpu_custom_call" | custom-call | tf_op jit(solution)/shard_map/pallas_call | solution.py:369
  16.4 2.0 %shard_map.65 = f32[1,4,16,8192]{3,2,1,0:T(8,128)} custom-call(f32[32,128]{1,0:T(8,128)S(1)} %get-tuple-element.8.mixed_ref, bf16[192,1024]{1,0:T(8,128)(2,1)S(1)} %get-tuple-element.9.table_ref, f32[1,8,32,128]{3,2,1,0:T(8,128)S(1)} %get-tuple-element.10.turn_ref), custom_call_target="tpu_custom_call" | custom-call | tf_op jit(solution)/shard_map/pallas_call | solution.py:396

commit v3 on v2

--- a/solution.py
+++ b/solution.py
@@ -230,7 +230,6 @@
     scatter(send2, recv2, 1)
 
     slab = groups * orders
-    levels = (steps - 1).bit_length()
 
     def put_tables(chunk, carry):
         column = jnp.concatenate(
@@ -256,11 +255,10 @@
         tall = 6 * slab
         table_ref[pl.ds(pl.multiple_of(chunk * tall, tall), tall), :] = jnp.concatenate(
             [table_high, table_high, table_low], axis=0)
-        for level in range(levels):
-            phase = column * (INNER << level)
-            sine = sin_turn(phase, turn)
-            turn_ref[chunk, 2 * level] = sin_turn(phase + turn // 4, turn)
-            turn_ref[chunk, 2 * level + 1] = jnp.where(place < LANES // 2, -sine, sine)
+        for pair in range(steps // 2):
+            phase = column * (INNER * (2 * pair + lax.div(place, LANES // 2)))
+            turn_ref[chunk, pair, 0] = sin_turn(phase + turn // 4, turn)
+            turn_ref[chunk, pair, 1] = sin_turn(phase, turn)
         return carry
 
     lax.fori_loop(0, blks // groups, put_tables, 0, unroll=blks == groups)
@@ -285,7 +283,9 @@
         mixed += along * value
         crossed += across * value
     mixed = mixed + pltpu.roll(crossed, LANES // 2, 1)
-    mixed_ref[...] = mixed
+    rolled = pltpu.roll(mixed, LANES // 2, 1)
+    mixed_ref[0] = jnp.where(half_lane, mixed, rolled)
+    mixed_ref[1] = jnp.where(half_lane, rolled, mixed)
 
     settle(recv1, send_sem, 0)
     settle(recv2, send_sem, 1)
@@ -294,27 +294,20 @@
 def maps_kernel(turn, maps, cycles, mixed_ref, table_ref, turn_ref, out_hbm, out_ref, total, out_sem):
     slab = 32
     steps = turn // INNER
-    chunks = mixed_ref.shape[0] // slab
-    lane = iota((slab, LANES), 1)
-    real = lane < LANES // 2
+    chunks = mixed_ref.shape[1] // slab
     writes = []
 
     def maps_of(chunk, last):
         tall = 6 * slab
         right = table_ref[pl.ds(pl.multiple_of(chunk * tall, tall), tall), :]
-        turns = [mixed_ref[pl.ds(chunk * slab, slab), :]]
-        while len(turns) < steps:
-            level = 2 * (len(turns).bit_length() - 1)
-            along, across = turn_ref[chunk, level], turn_ref[chunk, level + 1]
-            turns = turns + [
-                along * value + across * pltpu.roll(value, LANES // 2, 1) for value in turns
-            ]
+        rows = pl.ds(chunk * slab, slab)
+        mixed_real, mixed_imag = mixed_ref[0, rows, :], mixed_ref[1, rows, :]
         for pair in range(steps // 2):
-            one, two = turns[2 * pair], turns[2 * pair + 1]
+            cosine, sine = turn_ref[chunk, pair, 0], turn_ref[chunk, pair, 1]
             left = jnp.concatenate(
                 [
-                    jnp.where(real, one, pltpu.roll(two, LANES // 2, 1)),
-                    jnp.where(real, pltpu.roll(one, LANES // 2, 1), two),
+                    mixed_real * cosine - mixed_imag * sine,
+                    mixed_real * sine + mixed_imag * cosine,
                 ],
                 axis=0,
             )
@@ -326,8 +319,7 @@
                 total[pair] = value
             if last:
                 real_part, imag_part = value[:, :INNER], value[:, INNER:]
-                power = real_part * real_part + imag_part * imag_part
-                modulus = power * lax.rsqrt(jnp.maximum(power, 1e-37))
+                modulus = jnp.sqrt(real_part * real_part + imag_part * imag_part)
                 half = maps * cycles
                 for part in range(2):
                     a = 2 * pair + part
@@ -359,13 +351,12 @@
     orders = legendre.shape[0]
     vmem = pl.BlockSpec(memory_space=pltpu.VMEM)
     hbm = pl.BlockSpec(memory_space=pltpu.HBM)
-    slots = jax.ShapeDtypeStruct((blks * orders, LANES), jnp.float32)
+    slots = jax.ShapeDtypeStruct((2, blks * orders, LANES), jnp.float32)
     sky_map, legendre, wigner, wavelet, order_ids, dir_ids = (pltpu.with_memory_space_constraint(x, pltpu.HBM) for x in (sky_map, legendre, wigner, wavelet, order_ids, dir_ids))
     slab = LANES // cycles * orders
     chunks = blks * orders // slab
     table = jax.ShapeDtypeStruct((chunks * 6 * slab, 2 * INNER), jnp.bfloat16)
-    levels = (turn // INNER - 1).bit_length()
-    turns = jax.ShapeDtypeStruct((chunks, 2 * levels, slab, LANES), jnp.float32)
+    turns = jax.ShapeDtypeStruct((chunks, turn // INNER // 2, 2, slab, LANES), jnp.float32)
     middle = pl.pallas_call(
         functools.partial(spectra_kernel, blks, dirs),
         out_shape=(slots, table, turns),

time: 18.5 us -> 18.4 us (level)
  no operation moved by 1% of the time
where the time goes in v3:
time: 18.4 us; the launch traced here: 18.2 us
  Pallas kernels  18.2 us (99%)
    pallas_call x1, Pallas kernels, local(): pl.pallas_call(functools.partial(spectra_kernel, blks, dirs), out_shape=(...  16.4 us
    pallas_call x1, Pallas kernels, local(): pl.pallas_call(functools.partial(maps_kernel, turn, dirs, cycles), out_sh...  1.82 us

profile of v3, /device:TPU:0, one launch (start us, length us, event | category | flops | bytes accessed | tf_op | source)
XLA Modules:
  0.0 18.2 jit_solution(2277455742527791978)
XLA Ops:
  0.0 16.4 %shard_map.64 = (f32[2,32,128]{2,1,0:T(8,128)S(1)}, bf16[192,1024]{1,0:T(8,128)(2,1)S(1)}, f32[1,8,2,32,128]{4,3,2,1,0:T(8,128)S(1)}) custom-call(s32[32]{0:T(128)} %order_hbm.1, s32[4]{0:T(128)} %dir_hbm.1, f32[1,16,8192]{2,1,0:T(8,128)} %sky_hbm.1, f32[4,64,128]{2,1,0:T(8,128)} %legendre_hbm.1, f32[1,4,64,128]{3,2,1,0:T(8,128)} %wigner_hbm.1, ...), custom_call_target="tpu_custom_call" | custom-call | tf_op jit(solution)/shard_map/pallas_call | solution.py:360
  16.4 1.8 %shard_map.65 = f32[1,4,16,8192]{3,2,1,0:T(8,128)} custom-call(f32[2,32,128]{2,1,0:T(8,128)S(1)} %get-tuple-element.8.mixed_ref, bf16[192,1024]{1,0:T(8,128)(2,1)S(1)} %get-tuple-element.9.table_ref, f32[1,8,2,32,128]{4,3,2,1,0:T(8,128)S(1)} %get-tuple-element.10.turn_ref), custom_call_target="tpu_custom_call" | custom-call | tf_op jit(solution)/shard_map/pallas_call | solution.py:387

commit v4 on v3

--- a/solution.py
+++ b/solution.py
@@ -73,7 +73,7 @@
         return lax.div(other, dirs), lax.rem(other, dirs)
 
     def for_partners(body):
-        lax.fori_loop(1, devices, lambda step, carry: body(*partner(step)), None, unroll=1)
+        lax.fori_loop(1, devices, lambda step, carry: body(*partner(step)), None, unroll=devices <= 32)
 
     def greet(other_blk, other_dir):
         pl.semaphore_signal(
@@ -274,6 +274,7 @@
         sine = sin_turn(phase, turn)
         factors.append((sin_turn(phase + turn // 4, turn), jnp.where(half_lane, sine, -sine)))
 
+    settle(recv1, send_sem, 0)
     settle(recv2, recv_sem, 1)
 
     mixed = jnp.zeros((blks * orders, LANES), jnp.float32)
@@ -287,7 +288,6 @@
     mixed_ref[0] = jnp.where(half_lane, mixed, rolled)
     mixed_ref[1] = jnp.where(half_lane, rolled, mixed)
 
-    settle(recv1, send_sem, 0)
     settle(recv2, send_sem, 1)
 
 

time: 18.4 us -> 18.4 us (level)
  no operation moved by 1% of the time
where the time goes in v4:
time: 18.4 us; the launch traced here: 18.2 us
  Pallas kernels  18.2 us (99%)
    pallas_call x1, Pallas kernels, local(): pl.pallas_call(functools.partial(spectra_kernel, blks, dirs), out_shape=(...  16.4 us
    pallas_call x1, Pallas kernels, local(): pl.pallas_call(functools.partial(maps_kernel, turn, dirs, cycles), out_sh...  1.82 us

profile of v4, /device:TPU:0, one launch (start us, length us, event | category | flops | bytes accessed | tf_op | source)
XLA Modules:
  0.0 18.2 jit_solution(5789294433686967984)
XLA Ops:
  0.0 16.4 %shard_map.64 = (f32[2,32,128]{2,1,0:T(8,128)S(1)}, bf16[192,1024]{1,0:T(8,128)(2,1)S(1)}, f32[1,8,2,32,128]{4,3,2,1,0:T(8,128)S(1)}) custom-call(s32[32]{0:T(128)} %order_hbm.1, s32[4]{0:T(128)} %dir_hbm.1, f32[1,16,8192]{2,1,0:T(8,128)} %sky_hbm.1, f32[4,64,128]{2,1,0:T(8,128)} %legendre_hbm.1, f32[1,4,64,128]{3,2,1,0:T(8,128)} %wigner_hbm.1, ...), custom_call_target="tpu_custom_call" | custom-call | tf_op jit(solution)/shard_map/pallas_call | solution.py:360
  16.4 1.8 %shard_map.65 = f32[1,4,16,8192]{3,2,1,0:T(8,128)} custom-call(f32[2,32,128]{2,1,0:T(8,128)S(1)} %get-tuple-element.8.mixed_ref, bf16[192,1024]{1,0:T(8,128)(2,1)S(1)} %get-tuple-element.9.table_ref, f32[1,8,2,32,128]{4,3,2,1,0:T(8,128)S(1)} %get-tuple-element.10.turn_ref), custom_call_target="tpu_custom_call" | custom-call | tf_op jit(solution)/shard_map/pallas_call | solution.py:387

commit v5 on v3

--- a/solution.py
+++ b/solution.py
@@ -170,8 +170,10 @@
     for load in loads[2:]:
         load.wait()
     flat = orders * degrees
-    legendre_both = jnp.concatenate(halves(legendre_ref[...].reshape(flat, thetas)), axis=0)
+    legendre_high, legendre_low = halves(legendre_ref[...].reshape(flat, thetas))
+    legendre_both = jnp.concatenate([legendre_high, legendre_high, legendre_low], axis=1)
     wigner_high, wigner_low = halves(wigner_ref[0].reshape(flat, thetas))
+    wigner_both = jnp.concatenate([wigner_high, wigner_high, wigner_low], axis=0)
     tall = maps * rows
     own_ids = column_of(
         [order_ref[blk * orders + s] for s in range(orders)], iota((tall, flat), 0),
@@ -198,13 +200,10 @@
                 out = jnp.where(hit, turned, out)
             chunks.append(out)
         spectra.append(jnp.concatenate(chunks, axis=1))
-    both = jnp.concatenate(halves(jnp.concatenate(spectra, axis=0)), axis=0)
-    product = dot(both, legendre_both, ((1,), (1,)))
-    coeffs = product[:tall, :flat] + product[:tall, flat:] + product[tall:, :flat]
-    both = jnp.concatenate(halves(coeffs * weight), axis=0)
-    first = dot(both, wigner_high, ((1,), (0,)))
-    second = dot(both[:tall], wigner_low, ((1,), (0,)))
-    component = first[:tall] + first[tall:] + second
+    high, low = halves(jnp.concatenate(spectra, axis=0))
+    coeffs = dot(jnp.concatenate([high, low, high], axis=1), legendre_both, ((1,), (1,)))
+    high, low = halves(coeffs * weight)
+    component = dot(jnp.concatenate([high, low, high], axis=1), wigner_both, ((1,), (0,)))
 
     for h in range(thetas // LANES):
         turned = [

time: 18.4 us -> 18.4 us (level)
  no operation moved by 1% of the time
where the time goes in v5:
time: 18.4 us; the launch traced here: 18.3 us
  Pallas kernels  18.3 us (99%)
    pallas_call x1, Pallas kernels, local(): pl.pallas_call(functools.partial(spectra_kernel, blks, dirs), out_shape=(...  16.4 us
    pallas_call x1, Pallas kernels, local(): pl.pallas_call(functools.partial(maps_kernel, turn, dirs, cycles), out_sh...  1.83 us

profile of v5, /device:TPU:0, one launch (start us, length us, event | category | flops | bytes accessed | tf_op | source)
XLA Modules:
  0.0 18.3 jit_solution(13009670116200781342)
XLA Ops:
  0.0 16.4 %shard_map.64 = (f32[2,32,128]{2,1,0:T(8,128)S(1)}, bf16[192,1024]{1,0:T(8,128)(2,1)S(1)}, f32[1,8,2,32,128]{4,3,2,1,0:T(8,128)S(1)}) custom-call(s32[32]{0:T(128)} %order_hbm.1, s32[4]{0:T(128)} %dir_hbm.1, f32[1,16,8192]{2,1,0:T(8,128)} %sky_hbm.1, f32[4,64,128]{2,1,0:T(8,128)} %legendre_hbm.1, f32[1,4,64,128]{3,2,1,0:T(8,128)} %wigner_hbm.1, ...), custom_call_target="tpu_custom_call" | custom-call | tf_op jit(solution)/shard_map/pallas_call | solution.py:359
  16.4 1.8 %shard_map.65 = f32[1,4,16,8192]{3,2,1,0:T(8,128)} custom-call(f32[2,32,128]{2,1,0:T(8,128)S(1)} %get-tuple-element.8.mixed_ref, bf16[192,1024]{1,0:T(8,128)(2,1)S(1)} %get-tuple-element.9.table_ref, f32[1,8,2,32,128]{4,3,2,1,0:T(8,128)S(1)} %get-tuple-element.10.turn_ref), custom_call_target="tpu_custom_call" | custom-call | tf_op jit(solution)/shard_map/pallas_call | solution.py:386
